TPU v7x, 32 devices: a whole 2x2x4 slice. The times are simulated.
32 devices in a mesh: dp: 8 (over z, y), expert: 4 (over x, core).
Axes of the slice: x: 2, y: 2, z: 4, core: 2. Of those that a mesh axis runs over, the one named last changes fastest.
Arguments:
- tokens: bfloat16 [4096, 2048], P(('dp', 'expert')), may hold values from -6 to 6
- cotangent: bfloat16 [4096, 2048], P(('dp', 'expert')), may hold values from -6 to 6
- expert_ids: int32 [4096, 2], P(('dp', 'expert')), may hold values from 0 to 3, all different within a row; in each aligned block of 128 rows (0 to 127, 128 to 255, ...) at most 80 rows name the same one
- gate_probs: float32 [4096, 2], P(('dp', 'expert')), may hold values from 0.2 to 1
- gate_up_weight: bfloat16 [4, 2048, 1024], P('expert'), may hold values from -0.125 to 0.125
- down_weight: bfloat16 [4, 512, 2048], P('expert'), may hold values from -0.25 to 0.25
- down_residual: bfloat16 [8, 4, 512, 2048], P('dp', 'expert'), may hold values from -12 to 12
Outputs:
- token_grad: bfloat16 [4096, 2048], P(('dp', 'expert'))
- grad_gate_up: float32 [4, 2048, 1024], P('expert', 'dp')
- grad_down: float32 [4, 512, 2048], P('expert', 'dp')
Inputs may be any that keep to these rules, and one draw needn't show every extreme that they name: `expert_ids`: each token names 2 different experts. Among the tokens of one device no expert is named by more than 80 tokens, and in some device's tokens one expert is named by exactly 80.
All inputs are finite; a program needn't handle non-finite values.
Results may differ from a plain program's by a relative error of at most 0.0065.
Values may be sent and summed in bfloat16 or wider, within the bound.
No kernel may reach another device: no remote copies, remote signals or barrier semaphores. Data moves between devices by JAX's collectives and lax.ppermute only.
A program may use at most 128 MiB of HBM per device.

v0:
```python
import jax
import jax.numpy as jnp
from jax import lax
from jax.sharding import PartitionSpec as P


def expert_forward(token_rows, gate_up):
    hidden_units = gate_up.shape[1] // 2
    projected = jnp.dot(token_rows, gate_up, preferred_element_type=jnp.float32)
    gate_part = projected[:, :hidden_units]
    up_part = projected[:, hidden_units:]
    gate_sig = jax.nn.sigmoid(gate_part)
    activated = gate_part * gate_sig
    hidden = (activated * up_part).astype(jnp.bfloat16)
    return (gate_part, up_part, gate_sig, activated, hidden)


def expert_backward(token_rows, scaled, forward, gate_up, down_matrix):
    gate_part, up_part, gate_sig, activated, hidden = forward
    back_hidden = jnp.dot(scaled, down_matrix.T, preferred_element_type=jnp.float32)
    back_gate = back_hidden * up_part * gate_sig * (1.0 + gate_part * (1.0 - gate_sig))
    back_up = back_hidden * activated
    back_both = jnp.concatenate([back_gate, back_up], axis=1).astype(jnp.bfloat16)
    token_part = jnp.dot(back_both, gate_up.T, preferred_element_type=jnp.float32).astype(
        jnp.bfloat16
    )
    contract = (((0,), (0,)), ((), ()))
    gate_up_term = lax.dot_general(
        token_rows, back_both, contract, preferred_element_type=jnp.float32
    )
    down_term = lax.dot_general(hidden, scaled, contract, preferred_element_type=jnp.float32)
    return (token_part, gate_up_term, down_term)


def on_device(
    tokens, cotangent, expert_ids, gate_probs, gate_up_weight, down_weight, down_residual
):
    tok_rows, model_width = tokens.shape
    expert_count = lax.axis_size("expert")
    capacity = tok_rows * 5 // 8
    expert_range = jnp.arange(expert_count, dtype=jnp.int32)
    route_hit = expert_ids[:, :, None] == expert_range[None, None, :]
    member = jnp.any(route_hit, axis=1).astype(jnp.int32)
    route_weight = jnp.sum(jnp.where(route_hit, gate_probs[:, :, None], 0.0), axis=1)
    slot_index = jnp.cumsum(member, axis=0) - member
    slot_range = jnp.arange(capacity, dtype=jnp.int32)
    placed = (member.T[:, None, :] == 1) & (slot_index.T[:, None, :] == slot_range[None, :, None])
    token_range = jnp.arange(tok_rows, dtype=jnp.int32)
    filled = jnp.any(placed, axis=2)
    source_row = jnp.where(
        filled, jnp.sum(jnp.where(placed, token_range[None, None, :], 0), axis=2), tok_rows
    )
    slot_weight = jnp.sum(jnp.where(placed, route_weight.T[:, None, :], 0.0), axis=2)
    zero_row = jnp.zeros((1, model_width), jnp.bfloat16)
    send_rows = jnp.concatenate([tokens, zero_row], axis=0)[source_row]
    send_grads = (
        jnp.concatenate([cotangent, zero_row], axis=0)[source_row].astype(jnp.float32)
        * slot_weight[:, :, None]
    ).astype(jnp.bfloat16)
    gate_up = gate_up_weight[0]
    down_matrix = down_weight[0]
    total_rows = expert_count * capacity
    got_rows, got_grads = (
        lax.all_to_all(send_rows, "expert", split_axis=0, concat_axis=0, tiled=True),
        lax.all_to_all(send_grads, "expert", split_axis=0, concat_axis=0, tiled=True),
    )
    flat_rows = got_rows.reshape(total_rows, model_width)
    forward = expert_forward(flat_rows, gate_up)
    flat_grads = got_grads.reshape(total_rows, model_width)
    token_part, gate_up_term, down_term = expert_backward(
        flat_rows, flat_grads, forward, gate_up, down_matrix
    )
    returned = lax.all_to_all(
        token_part.reshape(expert_count, capacity, model_width),
        "expert",
        split_axis=0,
        concat_axis=0,
        tiled=True,
    )
    returned = returned.reshape(total_rows, model_width)
    pick_rows = expert_ids * capacity + jnp.take_along_axis(slot_index, expert_ids, axis=1)
    token_grad = jnp.sum(returned[pick_rows].astype(jnp.float32), axis=1).astype(jnp.bfloat16)
    gate_up_round = gate_up_term.astype(jnp.bfloat16)
    down_round = (down_term + down_residual[0, 0].astype(jnp.float32)).astype(jnp.bfloat16)
    group_count = lax.axis_size("dp")
    gate_up_wide = lax.optimization_barrier(gate_up_round).astype(jnp.float32)
    down_wide = lax.optimization_barrier(down_round).astype(jnp.float32)
    gate_up_part, down_part = (
        lax.psum_scatter(gate_up_wide, "dp", scatter_dimension=0, tiled=True),
        lax.psum_scatter(down_wide, "dp", scatter_dimension=0, tiled=True),
    )
    factor = 1.0 / group_count
    return (token_grad, (gate_up_part * factor)[None], (down_part * factor)[None])


def solution(mesh):
    placed = (
        P(("dp", "expert"), None),
        P(("dp", "expert"), None),
        P(("dp", "expert"), None),
        P(("dp", "expert"), None),
        P("expert", None, None),
        P("expert", None, None),
        P("dp", "expert", None, None),
    )
    return jax.shard_map(
        on_device,
        mesh=mesh,
        in_specs=placed,
        out_specs=(P(("dp", "expert"), None), P("expert", "dp", None), P("expert", "dp", None)),
        check_vma=False,
    )
```

profile of v0, /device:TPU:0, one launch (start us, length us, event | category | flops | bytes accessed | tf_op | source)
XLA Modules:
  0.0 313.3 jit_solution(13900823844935904877)
XLA Ops:
  7.2 0.8 fusion.15
  8.1 0.2 reduce_window_sum.11
  8.4 0.2 fusion.13
  8.6 0.2 select_reduce_fusion.1
  8.8 1.1 concatenate.11
  9.9 3.0 gather_fusion.1
  12.9 4.4 %all-to-all-start.1 = ((bf16[4,80,2048]{2,1,0:T(8,128)(2,1)}), bf16[4,80,2048]{2,1,0:T(8,128)(2,1)}, u32[]{:S(2)}, u32[]{:S(2)}) async-start(bf16[4,80,2048]{2,1,0:T(8,128)(2,1)} %bitcast.46), calls=%async_computation.1 | async-start | bytes 2621440 | tf_op jit(solution)/shard_map/all_to_all | solution.py:64
  17.4 3.0 gather_fusion
  20.5 0.1 select_reduce_fusion
  20.6 2.7 fusion.8
  23.3 12.0 %all-to-all-done.1 = bf16[4,80,2048]{2,1,0:T(8,128)(2,1)} async-done(((bf16[4,80,2048]{2,1,0:T(8,128)(2,1)}), bf16[4,80,2048]{2,1,0:T(8,128)(2,1)}, u32[]{:S(2)}, u32[]{:S(2)}) %all-to-all-start.1) | async-done | bytes 1310752 | tf_op jit(solution)/shard_map/all_to_all | solution.py:64
  35.3 3.5 %all-to-all-start = ((bf16[4,80,2048]{2,1,0:T(8,128)(2,1)}), bf16[4,80,2048]{2,1,0:T(8,128)(2,1)S(1)}, u32[]{:S(2)}, u32[]{:S(2)}) async-start(bf16[4,80,2048]{2,1,0:T(8,128)(2,1)} %fusion.8), calls=%async_computation | async-start | bytes 2621440 | tf_op jit(solution)/shard_map/all_to_all | solution.py:65
  38.9 5.2 %fusion.3 = f32[320,1024]{1,0:T(8,128)} fusion(bf16[320,2048]{1,0:T(8,128)(2,1)} %bitcast.8, bf16[1,2048,1024]{2,1,0:T(8,128)(2,1)} %param.11), kind=kOutput, calls=%fused_computation.8 | convolution fusion | flops 1342177280 | bytes 6815744 | tf_op jit(solution)/shard_map/dot_general | solution.py:9
  44.1 12.0 %all-to-all-done = bf16[4,80,2048]{2,1,0:T(8,128)(2,1)S(1)} async-done(((bf16[4,80,2048]{2,1,0:T(8,128)(2,1)}), bf16[4,80,2048]{2,1,0:T(8,128)(2,1)S(1)}, u32[]{:S(2)}, u32[]{:S(2)}) %all-to-all-start) | async-done | bytes 1310752 | tf_op jit(solution)/shard_map/all_to_all | solution.py:65
  56.1 3.4 %fusion = bf16[512,2048]{1,0:T(8,128)(2,1)S(1)} fusion(bf16[320,2048]{1,0:T(8,128)(2,1)S(1)} %bitcast.48, bf16[1,1,512,2048]{3,2,1,0:T(8,128)(2,1)} %param.13, f32[320,1024]{1,0:T(8,128)} %fusion.3), kind=kOutput, calls=%fused_computation.5 | convolution fusion | flops 675217408 | bytes 6815744 | tf_op jit(solution)/shard_map/dot_general | solution.py:31
  59.5 2.5 convert_element_type.49
  62.1 2.4 multiply_convert_fusion.2
  64.5 0.7 copy-done.4
  65.3 3.7 %convolution_convert_fusion = bf16[2048,1024]{1,0:T(8,128)(2,1)S(1)} fusion(bf16[320,2048]{1,0:T(8,128)(2,1)} %bitcast.8, bf16[320,512]{1,0:T(8,128)(2,1)S(1)} %get-tuple-element.4, bf16[320,512]{1,0:T(8,128)(2,1)S(1)} %get-tuple-element.3), kind=kOutput, calls=%fused_computation.10 | convolution fusion | flops 1345585152 | bytes 6160384 | tf_op jit(solution)/shard_map/dot_general | solution.py:28
  69.0 4.3 %convert_element_type.44 = f32[2048,1024]{1,0:T(8,128)} convert(bf16[2048,1024]{1,0:T(8,128)(2,1)S(1)} %convolution_convert_fusion) | non-fusion elementwise | flops 2097152 | bytes 12582912 | tf_op jit(solution)/shard_map/convert_element_type | solution.py:86
  73.3 0.9 copy-done.5
  74.3 4.9 %fusion.5 = bf16[320,2048]{1,0:T(8,128)(2,1)} fusion(bf16[1,2048,1024]{2,1,0:T(8,128)(2,1)} %param.11, bf16[320,512]{1,0:T(8,128)(2,1)S(1)} %copy-done.7, bf16[320,512]{1,0:T(8,128)(2,1)S(1)} %copy-done.5), kind=kOutput, calls=%fused_computation.11 | convolution fusion | flops 1344143360 | bytes 6160384 | tf_op jit(solution)/shard_map/dot_general | solution.py:24
  79.2 3.7 %all-to-all-start.2 = ((bf16[4,80,2048]{2,1,0:T(8,128)(2,1)}), bf16[4,80,2048]{2,1,0:T(8,128)(2,1)S(1)}, u32[]{:S(2)}, u32[]{:S(2)}) async-start(bf16[4,80,2048]{2,1,0:T(8,128)(2,1)} %bitcast.50), calls=%async_computation.2 | async-start | bytes 2621440 | tf_op jit(solution)/shard_map/all_to_all | solution.py:73
  83.2 2.4 gather_fusion.3
  86.1 13.9 %all-to-all-done.2 = bf16[4,80,2048]{2,1,0:T(8,128)(2,1)S(1)} async-done(((bf16[4,80,2048]{2,1,0:T(8,128)(2,1)}), bf16[4,80,2048]{2,1,0:T(8,128)(2,1)S(1)}, u32[]{:S(2)}, u32[]{:S(2)}) %all-to-all-start.2) | async-done | bytes 1310752 | tf_op jit(solution)/shard_map/all_to_all | solution.py:73
  100.0 2.3 gather_fusion.2
  102.3 1.7 reshape.85
  104.1 3.7 %reduce_sum.42 = bf16[128,2048]{1,0:T(8,128)(2,1)} reduce(bf16[128,2,2048]{2,1,0:T(2,128)(2,1)S(1)} %reshape.85, bf16[]{:T(256)} %constant.14.clone.1), dimensions={1}, to_apply=%region_6.7 | reduce | flops 262144 | bytes 1572866 | tf_op jit(solution)/shard_map/reduce_sum | solution.py:82
  107.8 43.4 %reduce-scatter.5.cloned.1.call-done = f32[64,2048]{1,0:T(8,128)} async-done(((f32[512,2048]{1,0:T(8,128)}), f32[64,2048]{1,0:T(8,128)}) %reduce-scatter.5.cloned.1.call-update) | async-done | bytes 524304 | tf_op jit(solution)/shard_map/reduce_scatter | solution.py:90
  151.2 1.9 multiply_bitcast_fusion.1
  153.1 151.1 %reduce-scatter.3.cloned.1.call-done = f32[256,1024]{1,0:T(8,128)} async-done(((f32[2048,1024]{1,0:T(8,128)}), f32[256,1024]{1,0:T(8,128)}) %reduce-scatter.3.cloned.1.call-update) | async-done | bytes 1048592 | tf_op jit(solution)/shard_map/reduce_scatter | solution.py:89
  304.1 2.3 multiply_bitcast_fusion
  (36 shorter events, 1.4 us)
Async XLA Ops:
  7.2 54.9 %copy-start = (bf16[1,512,2048]{2,1,0:T(8,128)(2,1)S(1)}, bf16[1,512,2048]{2,1,0:T(8,128)(2,1)}, u32[]{:S(2)}) copy-start(bf16[1,512,2048]{2,1,0:T(8,128)(2,1)} %param.12) | copy-start | bytes 6291460
  12.9 4.4 %copy-start.1 = (bf16[128,2048]{1,0:T(8,128)(2,1)S(1)}, bf16[128,2048]{1,0:T(8,128)(2,1)}, u32[]{:S(2)}) copy-start(bf16[128,2048]{1,0:T(8,128)(2,1)} %param.8) | copy-start | bytes 1572868
  12.9 22.4 %all-to-all-start.1 = ((bf16[4,80,2048]{2,1,0:T(8,128)(2,1)}), bf16[4,80,2048]{2,1,0:T(8,128)(2,1)}, u32[]{:S(2)}, u32[]{:S(2)}) async-start(bf16[4,80,2048]{2,1,0:T(8,128)(2,1)} %bitcast.46), calls=%async_computation.1 | async-start | bytes 2621440 | tf_op jit(solution)/shard_map/all_to_all | solution.py:64
  17.4 3.1 copy-start.2
  17.4 3.1 copy-start.3
  35.3 20.8 %all-to-all-start = ((bf16[4,80,2048]{2,1,0:T(8,128)(2,1)}), bf16[4,80,2048]{2,1,0:T(8,128)(2,1)S(1)}, u32[]{:S(2)}, u32[]{:S(2)}) async-start(bf16[4,80,2048]{2,1,0:T(8,128)(2,1)} %fusion.8), calls=%async_computation | async-start | bytes 2621440 | tf_op jit(solution)/shard_map/all_to_all | solution.py:65
  38.9 112.3 %reduce-scatter.5.cloned.1.call-start = ((), (), s32[]{:S(2)}) async-start(), calls=%async_computation.6 | async-start | bytes 4718592 | tf_op jit(solution)/shard_map/reduce_scatter | solution.py:90
  62.0 242.1 %reduce-scatter.3.cloned.1.call-start = ((), (), s32[]{:S(2)}) async-start(), calls=%async_computation.5 | async-start | bytes 9437184 | tf_op jit(solution)/shard_map/reduce_scatter | solution.py:89
  64.4 0.7 copy-start.4
  64.5 0.8 copy-start.6
  73.2 1.0 copy-start.5
  73.2 1.1 copy-start.7
  79.2 20.8 %all-to-all-start.2 = ((bf16[4,80,2048]{2,1,0:T(8,128)(2,1)}), bf16[4,80,2048]{2,1,0:T(8,128)(2,1)S(1)}, u32[]{:S(2)}, u32[]{:S(2)}) async-start(bf16[4,80,2048]{2,1,0:T(8,128)(2,1)} %bitcast.50), calls=%async_computation.2 | async-start | bytes 2621440 | tf_op jit(solution)/shard_map/all_to_all | solution.py:73
Sparse Core Ops, SparseCore 0:
  62.1 89.0 reduce-scatter.4
  155.3 148.8 reduce-scatter.2
where the time goes:
time: 314 us; the launch traced here: 313 us
  waiting for transfers between devices  232 us (74%)
  matrix products  19.5 us (6%)
  other arithmetic  18.9 us (6%)
  local copies, waits for them, and re-layouts  16.5 us (5%)
  between operations  14.2 us (5%)
  starting transfers between devices  11.8 us (4%)
    reduce_scatter x1, waiting for transfers between devices, on_device(): lax.psum_scatter(gate_up_wide, 'dp', scatter_dimension=0, tiled=True)  151 us
    reduce_scatter x1, waiting for transfers between devices, on_device(): lax.psum_scatter(down_wide, 'dp', scatter_dimension=0, tiled=True)  43.4 us
    all_to_all x1, waiting for transfers between devices, on_device(): lax.all_to_all(token_part.reshape(expert_count, capacity, model_width), '...  13.9 us
    all_to_all x1, waiting for transfers between devices, on_device(): lax.all_to_all(send_grads, 'expert', split_axis=0, concat_axis=0, tiled=T...  12 us
    all_to_all x1, waiting for transfers between devices, on_device(): lax.all_to_all(send_rows, 'expert', split_axis=0, concat_axis=0, tiled=True)  12 us
  transfers between devices with their start and end apart: 5, of which 5 were waited for; matrix products, arithmetic and copies ran while one was open for 12% of the time, Pallas kernels for 0%

commit v1 on v0

v1 whole, which is shorter than its diff:
```python
import jax
import jax.numpy as jnp
import numpy as np
from jax import lax
from jax.sharding import PartitionSpec as P

INNER = 2


def line_plan(length):
    orders = []
    for place in range(length):
        order = []
        for step in range(1, length):
            right, left = length - step + place, step - length + place
            if place < step and right not in order:
                order.append(right)
            if length - 1 - place < step and left not in order:
                order.append(left)
        order.append(place)
        orders.append(order)
    return np.array(orders, np.int32)


def flip(values, bit):
    count = lax.axis_size("expert")
    return lax.ppermute(values, "expert", [(i, i ^ bit) for i in range(count)])


def wide(values):
    return values.astype(jnp.float32)


def pick(candidates, slots, place):
    used = sorted({int(slot) for slot in slots if slot >= 0})
    chosen = candidates[used[0]]
    for slot in used[1:]:
        mask = np.array([s == slot for s in slots])
        chosen = jnp.where(jnp.asarray(mask)[place], candidates[slot], chosen)
    return chosen


def reduce_over_groups(chunk_of, group_count):
    length = group_count // INNER
    group = lax.axis_index("dp")
    place, side = group // INNER, group % INNER
    orders = line_plan(length)
    order_here = jnp.asarray(orders)[place]
    swap = [(i, i ^ 1) for i in range(group_count)]
    sums = []
    for slot in range(length):
        share = order_here[slot]
        sent = chunk_of(share * INNER + (1 - side))
        kept = chunk_of(share * INNER + side)
        sums.append(wide(kept) + wide(lax.ppermute(sent, "dp", swap)))
    slot_of = np.argsort(orders, axis=1)
    from_left = from_right = None
    for step in range(1, length):
        right_slots = [slot_of[p, length - step + p] if p < step else -1 for p in range(length)]
        left_slots = [
            slot_of[p, step - length + p] if length - 1 - p < step else -1 for p in range(length)
        ]
        to_right = pick(sums, right_slots, place)
        to_left = pick(sums, left_slots, place)
        if step > 1:
            to_right = to_right + wide(from_left)
            to_left = to_left + wide(from_right)
        right_pairs = [
            (p * INNER + s, (p + 1) * INNER + s) for p in range(step) for s in range(INNER)
        ]
        left_pairs = [
            (p * INNER + s, (p - 1) * INNER + s)
            for p in range(length - step, length)
            for s in range(INNER)
        ]
        from_left = lax.ppermute(to_right.astype(jnp.bfloat16), "dp", right_pairs)
        from_right = lax.ppermute(to_left.astype(jnp.bfloat16), "dp", left_pairs)
    return sums[-1] + wide(from_left) + wide(from_right)


def on_device(
    tokens, cotangent, expert_ids, gate_probs, gate_up_weight, down_weight, down_residual
):
    tok_rows, model_width = tokens.shape
    expert_count = lax.axis_size("expert")
    group_count = lax.axis_size("dp")
    gate_up, down_matrix = gate_up_weight[0], down_weight[0]
    hidden_units = down_matrix.shape[0]
    me = lax.axis_index("expert")
    expert_range = jnp.arange(expert_count, dtype=jnp.int32)
    route_hit = expert_ids[None, :, :] == expert_range[:, None, None]
    route = jnp.sum(jnp.where(route_hit, gate_probs[None, :, :], 0.0), axis=2)

    tokens_far = flip(tokens, 2)
    cotangent_far = flip(cotangent, 2)
    near_rows = jnp.concatenate([tokens, flip(tokens, 1)], axis=0)
    near_grads = jnp.concatenate([cotangent, flip(cotangent, 1)], axis=0)
    far_rows = jnp.concatenate([tokens_far, flip(tokens_far, 1)], axis=0)
    far_grads = jnp.concatenate([cotangent_far, flip(cotangent_far, 1)], axis=0)
    route_near = jnp.concatenate([route, flip(route, 1)], axis=1)
    route_all = jnp.concatenate([route_near, flip(route_near, 2)], axis=1)
    weight_here = lax.dynamic_index_in_dim(route_all, me, 0, keepdims=False)[:, None]

    def forward(rows):
        projected = jnp.dot(rows, gate_up, preferred_element_type=jnp.float32)
        gate_part, up_part = projected[:, :hidden_units], projected[:, hidden_units:]
        gate_sig = jax.nn.sigmoid(gate_part)
        activated = gate_part * gate_sig
        slope = up_part * gate_sig * (1.0 + gate_part * (1.0 - gate_sig))
        return (activated * up_part).astype(jnp.bfloat16), slope, activated

    def backward(grads, weight, slope, activated):
        scaled = (wide(grads) * weight).astype(jnp.bfloat16)
        back_hidden = jnp.dot(scaled, down_matrix.T, preferred_element_type=jnp.float32)
        back_both = jnp.concatenate([back_hidden * slope, back_hidden * activated], axis=1)
        return scaled, back_both.astype(jnp.bfloat16)

    near_count = near_rows.shape[0]
    hidden_near, slope_near, act_near = forward(near_rows)
    hidden_far, slope_far, act_far = forward(far_rows)
    scaled_near, back_near = backward(near_grads, weight_here[:near_count], slope_near, act_near)
    scaled_far, back_far = backward(far_grads, weight_here[near_count:], slope_far, act_far)
    all_rows = jnp.concatenate([near_rows, far_rows], axis=0)
    hidden = jnp.concatenate([hidden_near, hidden_far], axis=0)
    scaled = jnp.concatenate([scaled_near, scaled_far], axis=0)
    back_both = jnp.concatenate([back_near, back_far], axis=0)

    contract = (((0,), (0,)), ((), ()))
    gate_up_term = lax.dot_general(
        all_rows, back_both, contract, preferred_element_type=jnp.float32
    ).astype(jnp.bfloat16)
    down_term = lax.dot_general(hidden, scaled, contract, preferred_element_type=jnp.float32)
    down_term = (down_term + wide(down_residual[0, 0])).astype(jnp.bfloat16)
    gate_rows, down_rows = model_width // group_count, hidden_units // group_count
    width = 2 * hidden_units
    folds = model_width // width

    def chunk_of(share):
        gate_part = lax.dynamic_slice_in_dim(gate_up_term, share * gate_rows, gate_rows, 0)
        down_part = lax.dynamic_slice_in_dim(down_term, share * down_rows, down_rows, 0)
        parts = [down_part[:, f * width : (f + 1) * width] for f in range(folds)]
        return jnp.concatenate([gate_part, *parts], axis=0)

    total = reduce_over_groups(chunk_of, group_count) * (1.0 / group_count)
    grad_gate_up = total[:gate_rows]
    grad_down = jnp.concatenate(
        [total[gate_rows + f * down_rows : gate_rows + (f + 1) * down_rows] for f in range(folds)],
        axis=1,
    )

    token_part = jnp.dot(back_both, gate_up.T, preferred_element_type=jnp.float32).astype(
        jnp.bfloat16
    )
    blocks = token_part.reshape(expert_count, tok_rows, model_width)
    own, core, far, far_core = blocks[0], blocks[1], blocks[2], blocks[3]
    crossed = flip(jnp.stack([core, far_core]), 1)
    to_far = (wide(far) + wide(crossed[1])).astype(jnp.bfloat16)
    token_grad = (wide(own) + wide(crossed[0]) + wide(flip(to_far, 2))).astype(jnp.bfloat16)
    return (token_grad, grad_gate_up[None], grad_down[None])


def solution(mesh):
    placed = (
        P(("dp", "expert"), None),
        P(("dp", "expert"), None),
        P(("dp", "expert"), None),
        P(("dp", "expert"), None),
        P("expert", None, None),
        P("expert", None, None),
        P("dp", "expert", None, None),
    )
    return jax.shard_map(
        on_device,
        mesh=mesh,
        in_specs=placed,
        out_specs=(P(("dp", "expert"), None), P("expert", "dp", None), P("expert", "dp", None)),
        check_vma=False,
    )
```

time: 314 us -> 134 us (0.43)
  waiting for transfers between devices: 232 us -> 65.2 us
  starting transfers between devices: 11.8 us -> 33.2 us
  between operations: 14.2 us -> 3.69 us
  local copies, waits for them, and re-layouts: 16.5 us -> 6.63 us
  other arithmetic: 18.9 us -> 9.6 us
  matrix products: 19.5 us -> 15.3 us
    reduce_scatter x2 -> x0, waiting for transfers between devices: 194 us -> none  [the longest x1 151 us: on_device(): lax.psum_scatter(gate_up_wide, 'dp', scatter_dimension=0, tiled=True)]
    ppermute x0 -> x20, waiting for transfers between devices: none -> 65.2 us  [the longest x4 27.6 us: reduce_over_groups(): sums.append(wide(kept) + wide(lax.ppermute(sent, 'dp', swap)))]
    all_to_all x3 -> x0, waiting for transfers between devices: 37.9 us -> none  [the longest x1 13.9 us: on_device(): lax.all_to_all(token_part.reshape(expert_count, capacity, model_width), '...]
    ppermute x0 -> x20, starting transfers between devices: none -> 33.2 us  [the longest x3 17.2 us: reduce_over_groups(): from_left = lax.ppermute(to_right.astype(jnp.bfloat16), 'dp', right_pairs)]
    gather x9 -> x0, local copies, waits for them, and re-layouts: 12.9 us -> none  [the longest x2 4.07 us: on_device(): returned[pick_rows].astype(jnp.float32)]
    all_to_all x3 -> x0, starting transfers between devices: 11.7 us -> none  [the longest x1 4.41 us: on_device(): lax.all_to_all(send_rows, 'expert', split_axis=0, concat_axis=0, tiled=True)]
    dot_general x5 -> x7, matrix products: 19.5 us -> 15.3 us  [the longest x2 5.93 us: forward(): projected = jnp.dot(rows, gate_up, preferred_element_type=jnp.float32)]
    broadcast_in_dim x2 -> x1, other arithmetic: 4.18 us -> 0.83 us  [on_device(): return (token_grad, grad_gate_up[None], grad_down[None])]
  transfers between devices with their start and end apart: 5 -> 20, of which waited for: 5 -> 8; matrix products, arithmetic and copies ran while one was open for 12% -> 15% of each run, Pallas kernels for 0% -> 0%
where the time goes in v1:
time: 134 us
  waiting for transfers between devices  65.2 us (49%)
  starting transfers between devices  33.2 us (25%)
  matrix products  15.3 us (11%)
  other arithmetic  9.6 us (7%)
  local copies, waits for them, and re-layouts  6.63 us (5%)
  between operations  3.69 us (3%)
    ppermute x4, waiting for transfers between devices, reduce_over_groups(): sums.append(wide(kept) + wide(lax.ppermute(sent, 'dp', swap)))  27.6 us
    ppermute x3, starting transfers between devices, reduce_over_groups(): from_left = lax.ppermute(to_right.astype(jnp.bfloat16), 'dp', right_pairs)  17.2 us
    ppermute x10, waiting for transfers between devices, flip(): return lax.ppermute(values, 'expert', [(i, i ^ bit) for i in range(count)])  16.1 us
    ppermute x3, waiting for transfers between devices, reduce_over_groups(): from_right = lax.ppermute(to_left.astype(jnp.bfloat16), 'dp', left_pairs)  10.9 us
    ppermute x3, waiting for transfers between devices, reduce_over_groups(): from_left = lax.ppermute(to_right.astype(jnp.bfloat16), 'dp', right_pairs)  10.6 us
    ppermute x10, starting transfers between devices, flip(): return lax.ppermute(values, 'expert', [(i, i ^ bit) for i in range(count)])  7.79 us
    dot_general x2, matrix products, forward(): projected = jnp.dot(rows, gate_up, preferred_element_type=jnp.float32)  5.93 us
    ppermute x4, starting transfers between devices, reduce_over_groups(): sums.append(wide(kept) + wide(lax.ppermute(sent, 'dp', swap)))  5.33 us
  transfers between devices with their start and end apart: 20, of which 8 were waited for; matrix products, arithmetic and copies ran while one was open for 15% of the time, Pallas kernels for 0%

profile of v1, /device:TPU:0, one launch (start us, length us, event | category | flops | bytes accessed | tf_op | source)
XLA Modules:
  0.0 133.7 jit_solution(10571795520629807532)
XLA Ops:
  0.6 3.0 %collective-permute-start.6 = (bf16[128,2048]{1,0:T(8,128)(2,1)}, bf16[128,2048]{1,0:T(8,128)(2,1)}, u32[]{:S(2)}, u32[]{:S(2)}) collective-permute-start(bf16[128,2048]{1,0:T(8,128)(2,1)} %param.11), channel_id=1, source_target_pairs={{0,2},{1,3},{2,0},{3,1},{4,6},{5,7},{6,4},{7,5},{8,10},{9,11},{10,... | collective-permute-start | bytes 1572872 | tf_op jit(solution)/shard_map/ppermute | solution.py:27
  7.0 1.9 %collective-permute-start.2 = (f32[4,256]{1,0:T(4,128)S(1)}, f32[4,256]{1,0:T(4,128)S(1)}, u32[]{:S(2)}, u32[]{:S(2)}) collective-permute-start(f32[4,256]{1,0:T(4,128)S(1)} %pad_maximum_fusion.8), channel_id=1, source_target_pairs={{0,2},{1,3},{2,0},{3,1},{4,6},{5,7},{6,4},{7,5},{8,10},{9,11},{10,... | collective-permute-start | bytes 12296 | tf_op jit(solution)/shard_map/ppermute | solution.py:27
  11.0 16.1 %collective-permute-done.2 = f32[4,256]{1,0:T(4,128)S(1)} collective-permute-done((f32[4,256]{1,0:T(4,128)S(1)}, f32[4,256]{1,0:T(4,128)S(1)}, u32[]{:S(2)}, u32[]{:S(2)}) %collective-permute-start.2) | collective-permute-done | bytes 4128 | tf_op jit(solution)/shard_map/ppermute | solution.py:27
  27.7 1.3 multiply_convert_fusion.1
  29.0 3.6 %fusion.5 = f32[256,1024]{1,0:T(8,128)S(1)} fusion(bf16[1,2048,1024]{2,1,0:T(8,128)(2,1)} %param.15, bf16[128,2048]{1,0:T(8,128)(2,1)} %collective-permute-done.3, bf16[128,2048]{1,0:T(8,128)(2,1)S(1)} %copy-done.3), kind=kOutput, calls=%fused_computation.6 | convolution fusion | flops 1075838976 | bytes 6291456 | tf_op jit(solution)/shard_map/dot_general | solution.py:105
  32.7 1.0 multiply_convert_fusion.7
  33.7 1.1 copy-done.1
  34.9 2.3 %fusion.3 = f32[256,1024]{1,0:T(8,128)S(1)} fusion(bf16[1,2048,1024]{2,1,0:T(8,128)(2,1)S(1)} %copy-done.1, bf16[128,2048]{1,0:T(8,128)(2,1)S(1)} %collective-permute-done.7, bf16[128,2048]{1,0:T(8,128)(2,1)} %collective-permute-done.6), kind=kOutput, calls=%fused_computation.4 | convolution fusion | flops 1075838976 | bytes 6291456 | tf_op jit(solution)/shard_map/dot_general | solution.py:105
  37.4 1.0 multiply_convert_fusion.5
  39.0 1.3 %fusion = bf16[512,2048]{1,0:T(8,128)(2,1)S(1)} fusion(bf16[256,2048]{1,0:T(8,128)(2,1)S(1)} %multiply_convert_fusion, bf16[256,2048]{1,0:T(8,128)(2,1)S(1)} %multiply_convert_fusion.1, bf16[1,1,512,2048]{3,2,1,0:T(8,128)(2,1)S(1)} %copy-done.2, bf16[256,512]{1,0:T(8,128)(2,1)S(1)} %get-tuple-element.40, bf16[256,512]{1,0:T(8,128)(2,1)S(1)} %get-tuple-element.39), kind=kOutput, calls=%fused_computation.1 | convolution fusion | flops 1082130432 | bytes 6815744 | tf_op jit(solution)/shard_map/dot_general | solution.py:132
  40.4 3.6 %convolution_convert_fusion = bf16[2048,1024]{1,0:T(8,128)(2,1)S(1)} fusion(bf16[128,2048]{1,0:T(8,128)(2,1)S(1)} %collective-permute-done.7, bf16[128,2048]{1,0:T(8,128)(2,1)} %collective-permute-done.6, bf16[128,2048]{1,0:T(8,128)(2,1)} %collective-permute-done.3, bf16[128,2048]{1,0:T(8,128)(2,1)S(1)} %copy-done.3, ...), kind=kOutput, calls=%fused_computation.8 | convolution fusion | flops 2162163712 | bytes 7340032 | tf_op jit(solution)/shard_map/dot_general | solution.py:129
  44.9 1.8 %collective-permute-start.13 = (bf16[384,1024]{1,0:T(8,128)(2,1)S(1)}, bf16[384,1024]{1,0:T(8,128)(2,1)S(1)}, u32[]{:S(2)}, u32[]{:S(2)}) collective-permute-start(bf16[384,1024]{1,0:T(8,128)(2,1)S(1)} %pad_maximum_fusion.7), channel_id=1, source_target_pairs={{0,4},{4,0},{8,12},{12,8},{16,20},{20,16},{24,28},{28,24},{1,5},{5... | collective-permute-start | bytes 2359304 | tf_op jit(solution)/shard_map/ppermute | solution.py:55
  47.1 2.4 %fusion.7 = bf16[512,2048]{1,0:T(8,128)(2,1)S(1)} fusion(bf16[1,2048,1024]{2,1,0:T(8,128)(2,1)S(1)} %copy-done.1, bf16[256,512]{1,0:T(8,128)(2,1)S(1)} %get-tuple-element.38, bf16[256,512]{1,0:T(8,128)(2,1)S(1)} %get-tuple-element.37, bf16[256,512]{1,0:T(8,128)(2,1)S(1)} %get-tuple-element.36, bf16[256,512]{1,0:T(8,128)(2,1)S(1)} %get-tuple-element.35), kind=kOutput, calls=%fused_computation.9 | convolution fusion | flops 2152726528 | bytes 7340032 | tf_op jit(solution)/shard_map/dot_general | solution.py:151
  49.5 15.9 %collective-permute-done.13 = bf16[384,1024]{1,0:T(8,128)(2,1)S(1)} collective-permute-done((bf16[384,1024]{1,0:T(8,128)(2,1)S(1)}, bf16[384,1024]{1,0:T(8,128)(2,1)S(1)}, u32[]{:S(2)}, u32[]{:S(2)}) %collective-permute-start.13) | collective-permute-done | bytes 786464 | tf_op jit(solution)/shard_map/ppermute | solution.py:55
  65.7 3.8 %collective-permute-start.14 = (bf16[384,1024]{1,0:T(8,128)(2,1)S(1)}, bf16[384,1024]{1,0:T(8,128)(2,1)S(1)}, u32[]{:S(2)}, u32[]{:S(2)}) collective-permute-start(bf16[384,1024]{1,0:T(8,128)(2,1)S(1)} %fusion.24), channel_id=1, source_target_pairs={{0,8},{4,12},{1,9},{5,13},{2,10},{6,14},{3,11},{7,15}} | collective-permute-start | bytes 2359304 | tf_op jit(solution)/shard_map/ppermute | solution.py:76
  69.5 0.9 collective-permute-start.17
  72.3 1.6 %collective-permute-start.11 = (bf16[384,1024]{1,0:T(8,128)(2,1)S(1)}, bf16[384,1024]{1,0:T(8,128)(2,1)S(1)}, u32[]{:S(2)}, u32[]{:S(2)}) collective-permute-start(bf16[384,1024]{1,0:T(8,128)(2,1)S(1)} %pad_maximum_fusion.3), channel_id=1, source_target_pairs={{0,4},{4,0},{8,12},{12,8},{16,20},{20,16},{24,28},{28,24},{1,5},{5... | collective-permute-start | bytes 2359304 | tf_op jit(solution)/shard_map/ppermute | solution.py:55
  73.9 8.3 %collective-permute-done.12 = bf16[384,1024]{1,0:T(8,128)(2,1)S(1)} collective-permute-done((bf16[384,1024]{1,0:T(8,128)(2,1)S(1)}, bf16[384,1024]{1,0:T(8,128)(2,1)S(1)}, u32[]{:S(2)}, u32[]{:S(2)}) %collective-permute-start.12) | collective-permute-done | bytes 786464 | tf_op jit(solution)/shard_map/ppermute | solution.py:55
  82.2 2.5 %collective-permute-done.14 = bf16[384,1024]{1,0:T(8,128)(2,1)S(1)} collective-permute-done((bf16[384,1024]{1,0:T(8,128)(2,1)S(1)}, bf16[384,1024]{1,0:T(8,128)(2,1)S(1)}, u32[]{:S(2)}, u32[]{:S(2)}) %collective-permute-start.14) | collective-permute-done | bytes 786464 | tf_op jit(solution)/shard_map/ppermute | solution.py:76
  84.7 2.4 %add_convert_fusion.3 = (bf16[384,1024]{1,0:T(8,128)(2,1)S(1)}, bf16[384,1024]{1,0:T(8,128)(2,1)S(1)}) fusion(bf16[384,1024]{1,0:T(8,128)(2,1)S(1)} %collective-permute-done.14, bf16[384,1024]{1,0:T(8,128)(2,1)S(1)} %collective-permute-done.12, bf16[384,1024]{1,0:T(8,128)(2,1)S(1)} %collective-permute-done.13, pred[]{:T(512)} %bitcast.10, ...), kind=kLoop, calls=%fused_computation.30 | loop fusion | flops 9437184 | bytes 6291458 | tf_op jit(solution)/shard_map/convert_element_type | solution.py:76
  87.1 4.4 %collective-permute-start.15 = (bf16[384,1024]{1,0:T(8,128)(2,1)S(1)}, bf16[384,1024]{1,0:T(8,128)(2,1)S(1)}, u32[]{:S(2)}, u32[]{:S(2)}) collective-permute-start(bf16[384,1024]{1,0:T(8,128)(2,1)S(1)} %get-tuple-element.11), channel_id=1, source_target_pairs={{0,8},{4,12},{8,16},{12,20},{1,9},{5,13},{9,17},{13,21},{2,10},{6,... | collective-permute-start | bytes 2359304 | tf_op jit(solution)/shard_map/ppermute | solution.py:76
  92.4 1.6 %collective-permute-start.10 = (bf16[384,1024]{1,0:T(8,128)(2,1)S(1)}, bf16[384,1024]{1,0:T(8,128)(2,1)S(1)}, u32[]{:S(2)}, u32[]{:S(2)}) collective-permute-start(bf16[384,1024]{1,0:T(8,128)(2,1)S(1)} %pad_maximum_fusion.1), channel_id=1, source_target_pairs={{0,4},{4,0},{8,12},{12,8},{16,20},{20,16},{24,28},{28,24},{1,5},{5... | collective-permute-start | bytes 2359304 | tf_op jit(solution)/shard_map/ppermute | solution.py:55
  94.1 1.6 %collective-permute-start.9 = (bf16[128,2048]{1,0:T(8,128)(2,1)S(1)}, bf16[128,2048]{1,0:T(8,128)(2,1)S(1)}, u32[]{:S(2)}, u32[]{:S(2)}) collective-permute-start(bf16[128,2048]{1,0:T(8,128)(2,1)S(1)} %fusion.31), channel_id=1, source_target_pairs={{0,2},{1,3},{2,0},{3,1},{4,6},{5,7},{6,4},{7,5},{8,10},{9,11},{10,... | collective-permute-start | bytes 1572872 | tf_op jit(solution)/shard_map/ppermute | solution.py:27
  95.6 3.4 %collective-permute-done.11 = bf16[384,1024]{1,0:T(8,128)(2,1)S(1)} collective-permute-done((bf16[384,1024]{1,0:T(8,128)(2,1)S(1)}, bf16[384,1024]{1,0:T(8,128)(2,1)S(1)}, u32[]{:S(2)}, u32[]{:S(2)}) %collective-permute-start.11) | collective-permute-done | bytes 786464 | tf_op jit(solution)/shard_map/ppermute | solution.py:55
  99.1 6.9 %collective-permute-done.15 = bf16[384,1024]{1,0:T(8,128)(2,1)S(1)} collective-permute-done((bf16[384,1024]{1,0:T(8,128)(2,1)S(1)}, bf16[384,1024]{1,0:T(8,128)(2,1)S(1)}, u32[]{:S(2)}, u32[]{:S(2)}) %collective-permute-start.15) | collective-permute-done | bytes 786464 | tf_op jit(solution)/shard_map/ppermute | solution.py:76
  105.9 1.7 %add_convert_fusion.2 = (bf16[384,1024]{1,0:T(8,128)(2,1)S(1)}, bf16[384,1024]{1,0:T(8,128)(2,1)S(1)}) fusion(bf16[384,1024]{1,0:T(8,128)(2,1)S(1)} %collective-permute-done.15, bf16[384,1024]{1,0:T(8,128)(2,1)S(1)} %collective-permute-done.11, bf16[384,1024]{1,0:T(8,128)(2,1)S(1)} %collective-permute-done.12, pred[]{:T(512)} %bitcast.10, ...), kind=kLoop, calls=%fused_computation.29 | loop fusion | flops 9043968 | bytes 6291457 | tf_op jit(solution)/shard_map/convert_element_type | solution.py:76
  107.7 1.3 collective-permute-start.19
  109.0 9.0 %collective-permute-start.16 = (bf16[384,1024]{1,0:T(8,128)(2,1)S(1)}, bf16[384,1024]{1,0:T(8,128)(2,1)S(1)}, u32[]{:S(2)}, u32[]{:S(2)}) collective-permute-start(bf16[384,1024]{1,0:T(8,128)(2,1)S(1)} %get-tuple-element.33), channel_id=1, source_target_pairs={{0,8},{4,12},{8,16},{12,20},{16,24},{20,28},{1,9},{5,13},{9,17},{1... | collective-permute-start | bytes 2359304 | tf_op jit(solution)/shard_map/ppermute | solution.py:76
  118.0 1.0 fusion.33
  119.0 10.9 %collective-permute-done.19 = bf16[384,1024]{1,0:T(8,128)(2,1)S(1)} collective-permute-done((bf16[384,1024]{1,0:T(8,128)(2,1)S(1)}, bf16[384,1024]{1,0:T(8,128)(2,1)S(1)}, u32[]{:S(2)}, u32[]{:S(2)}) %collective-permute-start.19) | collective-permute-done | bytes 786464 | tf_op jit(solution)/shard_map/ppermute | solution.py:77
  130.0 1.2 collective-permute-done.16
  131.7 1.0 slice_bitcast_fusion
  (54 shorter events, 10.0 us)
Async XLA Ops:
  0.6 32.0 %copy-start = (bf16[1,512,2048]{2,1,0:T(8,128)(2,1)S(1)}, bf16[1,512,2048]{2,1,0:T(8,128)(2,1)}, u32[]{:S(2)}) copy-start(bf16[1,512,2048]{2,1,0:T(8,128)(2,1)} %param.16) | copy-start | bytes 6291460
  0.6 26.5 %collective-permute-start.6 = (bf16[128,2048]{1,0:T(8,128)(2,1)}, bf16[128,2048]{1,0:T(8,128)(2,1)}, u32[]{:S(2)}, u32[]{:S(2)}) collective-permute-start(bf16[128,2048]{1,0:T(8,128)(2,1)} %param.11), channel_id=1, source_target_pairs={{0,2},{1,3},{2,0},{3,1},{4,6},{5,7},{6,4},{7,5},{8,10},{9,11},{10,... | collective-permute-start | bytes 1572872 | tf_op jit(solution)/shard_map/ppermute | solution.py:27
  3.6 25.4 %collective-permute-start.3 = (bf16[128,2048]{1,0:T(8,128)(2,1)}, bf16[128,2048]{1,0:T(8,128)(2,1)}, u32[]{:S(2)}, u32[]{:S(2)}) collective-permute-start(bf16[128,2048]{1,0:T(8,128)(2,1)} %param.11), channel_id=1, source_target_pairs={{0,1},{1,0},{2,3},{3,2},{4,5},{5,4},{6,7},{7,6},{8,9},{9,8},{10,11... | collective-permute-start | bytes 1572872 | tf_op jit(solution)/shard_map/ppermute | solution.py:27
  3.7 23.6 %collective-permute-start.4 = (bf16[128,2048]{1,0:T(8,128)(2,1)}, bf16[128,2048]{1,0:T(8,128)(2,1)S(1)}, u32[]{:S(2)}, u32[]{:S(2)}) collective-permute-start(bf16[128,2048]{1,0:T(8,128)(2,1)} %param.12), channel_id=1, source_target_pairs={{0,2},{1,3},{2,0},{3,1},{4,6},{5,7},{6,4},{7,5},{8,10},{9,11},{10,... | collective-permute-start | bytes 1572872 | tf_op jit(solution)/shard_map/ppermute | solution.py:27
  3.8 23.9 %collective-permute-start = (bf16[128,2048]{1,0:T(8,128)(2,1)}, bf16[128,2048]{1,0:T(8,128)(2,1)S(1)}, u32[]{:S(2)}, u32[]{:S(2)}) collective-permute-start(bf16[128,2048]{1,0:T(8,128)(2,1)} %param.12), channel_id=1, source_target_pairs={{0,1},{1,0},{2,3},{3,2},{4,5},{5,4},{6,7},{7,6},{8,9},{9,8},{10,11... | collective-permute-start | bytes 1572872 | tf_op jit(solution)/shard_map/ppermute | solution.py:27
  4.9 2.1 %collective-permute-start.1 = (f32[4,128]{1,0:T(4,128)S(1)}, f32[4,128]{1,0:T(4,128)S(1)}, u32[]{:S(2)}, u32[]{:S(2)}) collective-permute-start(f32[4,128]{1,0:T(4,128)S(1)} %select_reduce_fusion), channel_id=1, source_target_pairs={{0,1},{1,0},{2,3},{3,2},{4,5},{5,4},{6,7},{7,6},{8,9},{9,8},{10,11... | collective-permute-start | bytes 6152 | tf_op jit(solution)/shard_map/ppermute | solution.py:27
  7.0 20.1 %collective-permute-start.2 = (f32[4,256]{1,0:T(4,128)S(1)}, f32[4,256]{1,0:T(4,128)S(1)}, u32[]{:S(2)}, u32[]{:S(2)}) collective-permute-start(f32[4,256]{1,0:T(4,128)S(1)} %pad_maximum_fusion.8), channel_id=1, source_target_pairs={{0,2},{1,3},{2,0},{3,1},{4,6},{5,7},{6,4},{7,5},{8,10},{9,11},{10,... | collective-permute-start | bytes 12296 | tf_op jit(solution)/shard_map/ppermute | solution.py:27
  11.0 18.0 %copy-start.3 = (bf16[128,2048]{1,0:T(8,128)(2,1)S(1)}, bf16[128,2048]{1,0:T(8,128)(2,1)}, u32[]{:S(2)}) copy-start(bf16[128,2048]{1,0:T(8,128)(2,1)} %param.11) | copy-start | bytes 1572868
  27.1 6.6 %collective-permute-start.7 = (bf16[128,2048]{1,0:T(8,128)(2,1)}, bf16[128,2048]{1,0:T(8,128)(2,1)S(1)}, u32[]{:S(2)}, u32[]{:S(2)}) collective-permute-start(bf16[128,2048]{1,0:T(8,128)(2,1)} %collective-permute-done.6), channel_id=1, source_target_pairs={{0,1},{1,0},{2,3},{3,2},{4,5},{5,4},{6,7},{7,6},{8,9},{9,8},{10,11... | collective-permute-start | bytes 1572872 | tf_op jit(solution)/shard_map/ppermute | solution.py:27
  27.2 10.0 %collective-permute-start.5 = (bf16[128,2048]{1,0:T(8,128)(2,1)S(1)}, bf16[128,2048]{1,0:T(8,128)(2,1)S(1)}, u32[]{:S(2)}, u32[]{:S(2)}) collective-permute-start(bf16[128,2048]{1,0:T(8,128)(2,1)S(1)} %collective-permute-done.4), channel_id=1, source_target_pairs={{0,1},{1,0},{2,3},{3,2},{4,5},{5,4},{6,7},{7,6},{8,9},{9,8},{10,11... | collective-permute-start | bytes 1572872 | tf_op jit(solution)/shard_map/ppermute | solution.py:27
  32.7 2.2 %copy-start.1 = (bf16[1,2048,1024]{2,1,0:T(8,128)(2,1)S(1)}, bf16[1,2048,1024]{2,1,0:T(8,128)(2,1)}, u32[]{:S(2)}) copy-start(bf16[1,2048,1024]{2,1,0:T(8,128)(2,1)} %param.15) | copy-start | bytes 12582916
  37.4 1.6 %copy-start.2 = (bf16[1,1,512,2048]{3,2,1,0:T(8,128)(2,1)S(1)}, bf16[1,1,512,2048]{3,2,1,0:T(8,128)(2,1)}, u32[]{:S(2)}) copy-start(bf16[1,1,512,2048]{3,2,1,0:T(8,128)(2,1)} %param.17) | copy-start | bytes 6291460
  44.9 20.5 %collective-permute-start.13 = (bf16[384,1024]{1,0:T(8,128)(2,1)S(1)}, bf16[384,1024]{1,0:T(8,128)(2,1)S(1)}, u32[]{:S(2)}, u32[]{:S(2)}) collective-permute-start(bf16[384,1024]{1,0:T(8,128)(2,1)S(1)} %pad_maximum_fusion.7), channel_id=1, source_target_pairs={{0,4},{4,0},{8,12},{12,8},{16,20},{20,16},{24,28},{28,24},{1,5},{5... | collective-permute-start | bytes 2359304 | tf_op jit(solution)/shard_map/ppermute | solution.py:55
  46.8 35.4 %collective-permute-start.12 = (bf16[384,1024]{1,0:T(8,128)(2,1)S(1)}, bf16[384,1024]{1,0:T(8,128)(2,1)S(1)}, u32[]{:S(2)}, u32[]{:S(2)}) collective-permute-start(bf16[384,1024]{1,0:T(8,128)(2,1)S(1)} %pad_maximum_fusion.5), channel_id=1, source_target_pairs={{0,4},{4,0},{8,12},{12,8},{16,20},{20,16},{24,28},{28,24},{1,5},{5... | collective-permute-start | bytes 2359304 | tf_op jit(solution)/shard_map/ppermute | solution.py:55
  65.7 19.1 %collective-permute-start.14 = (bf16[384,1024]{1,0:T(8,128)(2,1)S(1)}, bf16[384,1024]{1,0:T(8,128)(2,1)S(1)}, u32[]{:S(2)}, u32[]{:S(2)}) collective-permute-start(bf16[384,1024]{1,0:T(8,128)(2,1)S(1)} %fusion.24), channel_id=1, source_target_pairs={{0,8},{4,12},{1,9},{5,13},{2,10},{6,14},{3,11},{7,15}} | collective-permute-start | bytes 2359304 | tf_op jit(solution)/shard_map/ppermute | solution.py:76
  69.5 15.3 %collective-permute-start.17 = (bf16[384,1024]{1,0:T(8,128)(2,1)S(1)}, bf16[384,1024]{1,0:T(8,128)(2,1)S(1)}, u32[]{:S(2)}, u32[]{:S(2)}) collective-permute-start(bf16[384,1024]{1,0:T(8,128)(2,1)S(1)} %fusion.24), channel_id=1, source_target_pairs={{24,16},{28,20},{25,17},{29,21},{26,18},{30,22},{27,19},{31,23}} | collective-permute-start | bytes 2359304 | tf_op jit(solution)/shard_map/ppermute | solution.py:77
  70.4 0.7 copy-start.5
  70.4 1.2 copy-start.4
  70.6 23.4 %collective-permute-start.8 = (bf16[2,128,2048]{2,1,0:T(8,128)(2,1)S(1)}, bf16[2,128,2048]{2,1,0:T(8,128)(2,1)S(1)}, u32[]{:S(2)}, u32[]{:S(2)}) collective-permute-start(bf16[2,128,2048]{2,1,0:T(8,128)(2,1)S(1)} %pad_maximum_fusion), channel_id=1, source_target_pairs={{0,1},{1,0},{2,3},{3,2},{4,5},{5,4},{6,7},{7,6},{8,9},{9,8},{10,11... | collective-permute-start | bytes 3145736 | tf_op jit(solution)/shard_map/ppermute | solution.py:27
  72.3 26.7 %collective-permute-start.11 = (bf16[384,1024]{1,0:T(8,128)(2,1)S(1)}, bf16[384,1024]{1,0:T(8,128)(2,1)S(1)}, u32[]{:S(2)}, u32[]{:S(2)}) collective-permute-start(bf16[384,1024]{1,0:T(8,128)(2,1)S(1)} %pad_maximum_fusion.3), channel_id=1, source_target_pairs={{0,4},{4,0},{8,12},{12,8},{16,20},{20,16},{24,28},{28,24},{1,5},{5... | collective-permute-start | bytes 2359304 | tf_op jit(solution)/shard_map/ppermute | solution.py:55
  87.1 18.8 %collective-permute-start.15 = (bf16[384,1024]{1,0:T(8,128)(2,1)S(1)}, bf16[384,1024]{1,0:T(8,128)(2,1)S(1)}, u32[]{:S(2)}, u32[]{:S(2)}) collective-permute-start(bf16[384,1024]{1,0:T(8,128)(2,1)S(1)} %get-tuple-element.11), channel_id=1, source_target_pairs={{0,8},{4,12},{8,16},{12,20},{1,9},{5,13},{9,17},{13,21},{2,10},{6,... | collective-permute-start | bytes 2359304 | tf_op jit(solution)/shard_map/ppermute | solution.py:76
  91.6 14.4 %collective-permute-start.18 = (bf16[384,1024]{1,0:T(8,128)(2,1)S(1)}, bf16[384,1024]{1,0:T(8,128)(2,1)S(1)}, u32[]{:S(2)}, u32[]{:S(2)}) collective-permute-start(bf16[384,1024]{1,0:T(8,128)(2,1)S(1)} %get-tuple-element.12), channel_id=1, source_target_pairs={{16,8},{20,12},{24,16},{28,20},{17,9},{21,13},{25,17},{29,21},{18,... | collective-permute-start | bytes 2359304 | tf_op jit(solution)/shard_map/ppermute | solution.py:77
  92.4 26.7 %collective-permute-start.10 = (bf16[384,1024]{1,0:T(8,128)(2,1)S(1)}, bf16[384,1024]{1,0:T(8,128)(2,1)S(1)}, u32[]{:S(2)}, u32[]{:S(2)}) collective-permute-start(bf16[384,1024]{1,0:T(8,128)(2,1)S(1)} %pad_maximum_fusion.1), channel_id=1, source_target_pairs={{0,4},{4,0},{8,12},{12,8},{16,20},{20,16},{24,28},{28,24},{1,5},{5... | collective-permute-start | bytes 2359304 | tf_op jit(solution)/shard_map/ppermute | solution.py:55
  94.1 23.9 %collective-permute-start.9 = (bf16[128,2048]{1,0:T(8,128)(2,1)S(1)}, bf16[128,2048]{1,0:T(8,128)(2,1)S(1)}, u32[]{:S(2)}, u32[]{:S(2)}) collective-permute-start(bf16[128,2048]{1,0:T(8,128)(2,1)S(1)} %fusion.31), channel_id=1, source_target_pairs={{0,2},{1,3},{2,0},{3,1},{4,6},{5,7},{6,4},{7,5},{8,10},{9,11},{10,... | collective-permute-start | bytes 1572872 | tf_op jit(solution)/shard_map/ppermute | solution.py:27
  107.7 22.3 %collective-permute-start.19 = (bf16[384,1024]{1,0:T(8,128)(2,1)S(1)}, bf16[384,1024]{1,0:T(8,128)(2,1)S(1)}, u32[]{:S(2)}, u32[]{:S(2)}) collective-permute-start(bf16[384,1024]{1,0:T(8,128)(2,1)S(1)} %get-tuple-element.34), channel_id=1, source_target_pairs={{8,0},{12,4},{16,8},{20,12},{24,16},{28,20},{9,1},{13,5},{17,9},{2... | collective-permute-start | bytes 2359304 | tf_op jit(solution)/shard_map/ppermute | solution.py:77
  109.0 22.1 %collective-permute-start.16 = (bf16[384,1024]{1,0:T(8,128)(2,1)S(1)}, bf16[384,1024]{1,0:T(8,128)(2,1)S(1)}, u32[]{:S(2)}, u32[]{:S(2)}) collective-permute-start(bf16[384,1024]{1,0:T(8,128)(2,1)S(1)} %get-tuple-element.33), channel_id=1, source_target_pairs={{0,8},{4,12},{8,16},{12,20},{16,24},{20,28},{1,9},{5,13},{9,17},{1... | collective-permute-start | bytes 2359304 | tf_op jit(solution)/shard_map/ppermute | solution.py:76
